TPU v7x, 256 devices: a whole 4x4x8 slice. The times are simulated.
256 devices in a mesh: gz: 8 (over y, z_lo), row: 4 (over z_hi), col: 8 (over x, core).
Axes of the slice: x: 4, y: 4, z: 8 (z_hi: 4, z_lo: 2; z = z_hi * 2 + z_lo), core: 2. Of those that a mesh axis runs over, the one named last changes fastest.
Arguments:
- lower_sub: bfloat16 [8, 2048, 8192], P('gz', 'row'), may hold values from -0.0625 to 0.0625
- upper_sub: bfloat16 [8, 8192, 2048], P('gz', None, 'col'), may hold values from -6 to 6
- block_mask: int32 [8, 16, 16], P('gz', 'row', 'col'), may hold values 0 or 1
- front_base: float32 [2048, 2048], P(('row', 'gz'), 'col'), may hold values from -6 to 6
- pivot_inverse: float32 [2, 256, 256], replicated, may hold values from -0.01 to 0.01
- pivot_order: int32 [2, 256], replicated, may hold values from 0 to 255, each once within a row
Outputs:
- factored: float32 [2048, 2048], P(('row', 'gz'), 'col')
Inputs may be any that keep to these rules, and one draw needn't show every extreme that they name: Each row of pivot_order is a permutation of 0 .. 255.
All inputs are finite; a program needn't handle non-finite values. No bound on the sum of `block_mask` on one device may be relied on, other than what follows from the above.
Results may differ from a plain program's by a relative error of at most 0.0003.
Values sent between devices are 32-bit elements; how exact they have to be, the bound alone decides.
A program may use at most 64 MiB of HBM per device.

v0:
```python
import jax
import jax.numpy as jnp
from jax import lax
from jax.sharding import PartitionSpec as P


def spread_2(block, axis, holder):
    block = jnp.where(lax.axis_index(axis) == holder, block, jnp.zeros_like(block))
    return lax.psum(block, axis)


def on_device(lower_sub, upper_sub, block_mask, front_base, pivot_inverse, pivot_order):
    highest = lax.Precision.HIGHEST
    left_factor = lower_sub[0]
    right_factor = upper_sub[0]
    slab_rows = left_factor.shape[0]
    own_rows, own_cols = front_base.shape
    tiles = block_mask[0].astype(jnp.float32)
    tile_rows = slab_rows // tiles.shape[0]
    tile_cols = own_cols // tiles.shape[1]
    spread = jnp.broadcast_to(
        tiles[:, None, :, None], (tiles.shape[0], tile_rows, tiles.shape[1], tile_cols)
    ).reshape(slab_rows, own_cols)
    summed = lax.psum_scatter(
        jnp.dot(left_factor, right_factor, preferred_element_type=jnp.float32) * spread,
        "gz",
        scatter_dimension=0,
        tiled=True,
    )
    front = front_base + summed
    block_index = lax.axis_index("row") * lax.axis_size("gz") + lax.axis_index("gz")
    row_ids = block_index * own_rows + jnp.arange(own_rows, dtype=jnp.int32)
    col_ids = lax.axis_index("col") * own_cols + jnp.arange(own_cols, dtype=jnp.int32)
    panel_width = pivot_inverse.shape[1]
    for panel in range(pivot_inverse.shape[0]):
        start_row = panel * panel_width
        after_row = start_row + panel_width
        targets = start_row + jnp.arange(panel_width, dtype=jnp.int32)
        placer = (targets[:, None] == row_ids[None, :]).astype(jnp.float32)
        owned = (row_ids >= start_row) & (row_ids < after_row)
        column_rows = lax.all_gather(front, "gz", axis=0, tiled=True)
        pivot_block = spread_2(column_rows[start_row:after_row], "row", 0)
        permuted = jnp.take(pivot_block, pivot_order[panel], axis=0)
        placed = jnp.dot(placer.T, permuted, precision=highest)
        front = jnp.where(owned[:, None], placed, front)
        root_col = start_row // own_cols
        offset = start_row - root_col * own_cols
        panel_cols = front
        beneath = row_ids >= after_row
        lower = jnp.where(
            beneath[:, None], jnp.dot(panel_cols, pivot_inverse[panel], precision=highest), 0.0
        )
        lower = spread_2(lower, "col", root_col)
        is_root = lax.axis_index("col") == root_col
        front = front.at[:, offset : offset + panel_width].set(
            jnp.where(beneath[:, None] & is_root, lower, panel_cols)
        )
        update = jnp.dot(lower, permuted, precision=highest)
        front = front - jnp.where((col_ids >= after_row)[None, :], update, 0.0)
    return front


def solution(mesh):
    placed = (
        P("gz", "row", None),
        P("gz", None, "col"),
        P("gz", "row", "col"),
        P(("row", "gz"), "col"),
        P(),
        P(),
    )
    return jax.shard_map(
        on_device, mesh=mesh, in_specs=placed, out_specs=P(("row", "gz"), "col"), check_vma=False
    )
```

profile of v0, /device:TPU:68, one launch (start us, length us, event | category | flops | bytes accessed | tf_op | source)
XLA Modules:
  0.0 356.9 jit_solution(12610471177662328038)
XLA Ops:
  6.5 0.0 reduce-scatter.2.cloned.1.call-start
  6.5 0.7 convert_bitcast_fusion
  7.2 0.1 copy.7
  7.3 0.2 broadcast_in_dim.90
  7.5 0.0 copy-start.2
  7.5 0.0 copy-start.1
  7.5 0.0 copy-start
  7.6 7.8 %fusion.3 = f32[512,256]{1,0:T(8,128)} fusion(bf16[1,8192,256]{2,1,0:T(8,128)(2,1)} %param.17, bf16[1,512,8192]{2,1,0:T(8,128)(2,1)} %param.16, f32[64,8,2,128]{3,2,1,0:T(2,128)S(1)} %bitcast.28), kind=kOutput, calls=%fused_computation.5 | convolution fusion | flops 2147614720 | bytes 13631488 | tf_op jit(solution)/shard_map/dot_general | solution.py:25
  15.3 0.0 reduce-scatter.2.cloned.1.call-update
  15.3 0.0 all-reduce.5.cloned.1.call-start
  15.5 0.0 copy-done.2
  15.5 43.0 %reduce-scatter.2.cloned.1.call-done = f32[64,256]{1,0:T(8,128)} async-done(((f32[512,256]{1,0:T(8,128)}), f32[64,256]{1,0:T(8,128)}) %reduce-scatter.2.cloned.1.call-update) | async-done | bytes 65552 | tf_op jit(solution)/shard_map/reduce_scatter | solution.py:24
  58.5 0.0 copy-done.1
  58.5 0.8 add.81
  59.4 30.0 %all_gather.6 = f32[512,256]{1,0:T(8,128)S(1)} all-gather(f32[64,256]{1,0:T(8,128)S(1)} %add.81), channel_id=1, replica_groups=mesh['gz'=8,'row'=4,'col'=8] {'gz'}, dimensions={0}, use_global_device_ids=true | all-gather | bytes 589824 | tf_op jit(solution)/shard_map/all_gather | solution.py:41
  89.3 0.7 slice_select_fusion.1
  90.1 0.0 all-reduce.5.cloned.1.call-update
  90.1 0.0 all-reduce.7.cloned.1.call-start
  90.2 49.1 %all-reduce.5.cloned.1.call-done = f32[256,256]{1,0:T(8,128)} async-done(((f32[256,256]{1,0:T(8,128)}), f32[256,256]{1,0:T(8,128)}) %all-reduce.5.cloned.1.call-update) | async-done | bytes 262160 | tf_op jit(solution)/shard_map/psum | solution.py:9
  139.3 1.9 gather_fusion
  141.2 0.3 convolution_select_fusion.5
  141.5 0.0 copy-done
  141.5 0.9 fusion.11
  142.4 0.0 all-reduce.7.cloned.1.call-update
  142.4 0.0 all-reduce.9.cloned.1.call-start
  142.5 59.0 %all-reduce.7.cloned.1.call-done = f32[64,256]{1,0:T(8,128)} async-done(((f32[64,256]{1,0:T(8,128)}), f32[64,256]{1,0:T(8,128)}) %all-reduce.7.cloned.1.call-update) | async-done | bytes 65552 | tf_op jit(solution)/shard_map/psum | solution.py:9
  201.5 1.3 fusion.10
  202.8 30.1 %all_gather.7 = f32[512,256]{1,0:T(8,128)S(1)} all-gather(f32[64,256]{1,0:T(8,128)S(1)} %fusion.10), channel_id=1, replica_groups=mesh['gz'=8,'row'=4,'col'=8] {'gz'}, dimensions={0}, use_global_device_ids=true | all-gather | bytes 589824 | tf_op jit(solution)/shard_map/all_gather | solution.py:41
  232.9 0.7 slice_select_fusion
  233.6 0.0 all-reduce.9.cloned.1.call-update
  233.6 0.0 all-reduce.11.cloned.1.call-start
  233.7 52.4 %all-reduce.9.cloned.1.call-done = f32[256,256]{1,0:T(8,128)} async-done(((f32[256,256]{1,0:T(8,128)}), f32[256,256]{1,0:T(8,128)}) %all-reduce.9.cloned.1.call-update) | async-done | bytes 262160 | tf_op jit(solution)/shard_map/psum | solution.py:9
  286.1 1.9 gather_fusion.1
  288.1 0.4 convolution_select_fusion.2
  288.4 0.9 fusion.9
  289.3 0.0 all-reduce.11.cloned.1.call-update
  289.4 59.1 %all-reduce.11.cloned.1.call-done = f32[64,256]{1,0:T(8,128)} async-done(((f32[64,256]{1,0:T(8,128)}), f32[64,256]{1,0:T(8,128)}) %all-reduce.11.cloned.1.call-update) | async-done | bytes 65552 | tf_op jit(solution)/shard_map/psum | solution.py:9
  348.5 1.9 fusion.8
  (16 shorter events, 0.1 us)
Async XLA Ops:
  6.5 52.0 %reduce-scatter.2.cloned.1.call-start = ((), (), s32[]{:S(2)}) async-start(), calls=%async_computation.1 | async-start | bytes 589824 | tf_op jit(solution)/shard_map/reduce_scatter | solution.py:24
  7.5 8.0 %copy-start.2 = (s32[2,256]{1,0:T(2,128)S(1)}, s32[2,256]{1,0:T(2,128)}, u32[]{:S(2)}) copy-start(s32[2,256]{1,0:T(2,128)} %param.21) | copy-start | bytes 6148
  7.5 51.0 %copy-start.1 = (f32[64,256]{1,0:T(8,128)S(1)}, f32[64,256]{1,0:T(8,128)}, u32[]{:S(2)}) copy-start(f32[64,256]{1,0:T(8,128)} %param.19) | copy-start | bytes 196612
  7.5 134.0 %copy-start = (f32[2,256,256]{2,1,0:T(8,128)S(1)}, f32[2,256,256]{2,1,0:T(8,128)}, u32[]{:S(2)}) copy-start(f32[2,256,256]{2,1,0:T(8,128)} %param.20) | copy-start | bytes 1572868
  15.3 123.9 %all-reduce.5.cloned.1.call-start = ((), (), s32[]{:S(2)}) async-start(), calls=%async_computation.2 | async-start | bytes 524288 | tf_op jit(solution)/shard_map/psum | solution.py:9
  90.1 111.5 %all-reduce.7.cloned.1.call-start = ((), (), s32[]{:S(2)}) async-start(), calls=%async_computation.3 | async-start | bytes 131072 | tf_op jit(solution)/shard_map/psum | solution.py:9
  142.4 143.7 %all-reduce.9.cloned.1.call-start = ((), (), s32[]{:S(2)}) async-start(), calls=%async_computation.4 | async-start | bytes 524288 | tf_op jit(solution)/shard_map/psum | solution.py:9
  233.6 114.8 %all-reduce.11.cloned.1.call-start = ((), (), s32[]{:S(2)}) async-start(), calls=%async_computation.5 | async-start | bytes 131072 | tf_op jit(solution)/shard_map/psum | solution.py:9
Sparse Core Ops, SparseCore 0:
  15.5 43.0 reduce-scatter.1
  90.2 49.0 all-reduce.4
  142.6 58.9 all-reduce.6
  233.7 52.3 all-reduce.8
  289.5 58.9 all-reduce.10
where the time goes:
time: 362 us; the launch traced here: 357 us
  waiting for transfers between devices  263 us (73%)
  blocking collectives  60 us (17%)
  matrix products  13.4 us (4%)
  between operations  13.3 us (4%)
  local copies, waits for them, and re-layouts  4.15 us (1%)
    psum x4, waiting for transfers between devices, spread_2(): return lax.psum(block, axis)  220 us
    all_gather x2, blocking collectives, on_device(): column_rows = lax.all_gather(front, 'gz', axis=0, tiled=True)  60 us
    reduce_scatter x1, waiting for transfers between devices, on_device(): lax.psum_scatter(jnp.dot(left_factor, right_factor, preferred_element_typ...  43 us
    dot_general x1, matrix products, on_device(): jnp.dot(left_factor, right_factor, preferred_element_type=jnp.float32)  7.75 us
  transfers between devices with their start and end apart: 5, of which 5 were waited for; matrix products, arithmetic and copies ran while one was open for 0% of the time, Pallas kernels for 0%

commit v1 on v0

v1 whole, which is shorter than its diff:
```python
import functools

import jax
import jax.numpy as jnp
from jax import lax
from jax.experimental import pallas as pl
from jax.experimental.pallas import tpu as pltpu
from jax.sharding import PartitionSpec as P

F32 = jnp.float32
BF16 = jnp.bfloat16
MESH = pl.DeviceIdType.MESH


def split(x):
    hi = x.astype(BF16)
    return hi, (x - hi.astype(F32)).astype(BF16)


def dot(a, b):
    return jnp.dot(a, b, preferred_element_type=F32)


def dot3(x, w_hi, w_lo):
    hi, lo = split(x)
    n = x.shape[0]
    both = dot(jnp.concatenate([hi, lo], axis=0), w_hi)
    return both[:n] + (both[n:] + dot(hi, w_lo))


def kernel(
    ng, nr, nc, steps,
    a_hbm, b_hbm, mask_ref, base_ref, inv_ref, order_v, order_s,
    out_ref,
    a_v, b_v, part, land, own, f0, f1, x0, x1, m_hi, m_lo,
    a_sem, b_sem, rs_send, rs_recv,
    z_send, z_recv, ag_send, ag_recv, x_send, x_recv,
):
    g, r, c = lax.axis_index("gz"), lax.axis_index("row"), lax.axis_index("col")
    bs = inv_ref.shape[1]
    rows = own.shape[0]
    ch = rows // 2
    depth = a_v.shape[3]
    mb = bs // (mask_ref.shape[1] // 2)
    first = r == 0

    def a_copy(h, k):
        return pltpu.make_async_copy(
            a_hbm.at[0, pl.ds(h * bs, bs), pl.ds(k * depth, depth)], a_v.at[h, k], a_sem.at[h, k]
        )

    def b_copy(k):
        return pltpu.make_async_copy(b_hbm.at[0, pl.ds(k * depth, depth), :], b_v.at[k], b_sem.at[k])

    for k in range(steps):
        a_copy(0, k).start()
        b_copy(k).start()
    for k in range(steps):
        a_copy(1, k).start()

    barrier = pltpu.get_barrier_semaphore()

    def greet(axis, me, n):
        @pl.loop(1, n)
        def _(d):
            pl.semaphore_signal(barrier, inc=1, device_id={axis: lax.rem(me + d, n)}, device_id_type=MESH)

    greet("gz", g, ng)
    greet("row", r, nr)
    greet("col", c, nc)

    for p in range(2):
        placer = (lax.broadcasted_iota(jnp.int32, (bs, bs), 0) == order_v[p : p + 1, :]).astype(BF16)
        for plain, ref in zip(split(inv_ref[p]), (m_hi, m_lo)):
            moved = lax.dot_general(plain, placer, (((1,), (1,)), ((), ())), preferred_element_type=F32)
            ref[p] = jnp.where(c == p, plain.astype(F32), moved).astype(BF16)

    def rs_copy(p, i):
        q = p * ng + i
        dest = jnp.where(first, i, q // 2)
        h = jnp.where(first, p, q % 2)
        return dest, pltpu.make_async_remote_copy(
            src_ref=part.at[pl.ds(pl.multiple_of(p * bs + i * ch, ch), ch), :],
            dst_ref=land.at[h, g],
            send_sem=rs_send.at[p, i],
            recv_sem=rs_recv.at[h, g],
            device_id={"gz": dest},
            device_id_type=MESH,
        )

    for p in range(2):
        top = p * bs
        for k in range(steps):
            if p == 0:
                b_copy(k).wait()
            a_copy(p, k).wait()
            term = dot(a_v[p, k], b_v[k])
            if k == 0:
                part[top : top + bs, :] = term
            else:
                part[top : top + bs, :] += term
        for i in range(bs // mb):
            for j in range(bs // mb):
                at = (slice(top + i * mb, top + (i + 1) * mb), slice(j * mb, (j + 1) * mb))
                part[at] = part[at] * mask_ref[0, p * (bs // mb) + i, j].astype(F32)

        @pl.when(g // (ng // 2) == p)
        def _():
            mine = pl.ds(pl.multiple_of(g * rows, rows), rows)
            part[mine, :] = part[mine, :] + base_ref[...]

        if p == 0:
            pl.semaphore_wait(barrier, ng + nr + nc - 3)

        @pl.loop(0, ng)
        def _(d):
            i = lax.rem(d + g, ng)
            dest, copy = rs_copy(p, i)

            @pl.when(dest != g)
            def _():
                copy.start()

    def gather_copy(buf, n, d):
        return pltpu.make_async_remote_copy(
            src_ref=buf.at[g],
            dst_ref=buf.at[g],
            send_sem=ag_send.at[n, d],
            recv_sem=ag_recv.at[n, g],
            device_id={"gz": lax.rem(g + d, ng)},
            device_id_type=MESH,
        )

    def down_copy(buf, n, d):
        return pltpu.make_async_remote_copy(
            src_ref=buf.at[g],
            dst_ref=buf.at[g],
            send_sem=z_send.at[n, d],
            recv_sem=z_recv.at[n],
            device_id={"row": d},
            device_id_type=MESH,
        )

    def share(buf, n):
        @pl.when(first & (c > n))
        def _():
            @pl.loop(1, nr)
            def _(d):
                down_copy(buf, n, d).start()

        @pl.when(jnp.logical_not(first) & (c > n))
        def _():
            down_copy(buf, n, 1).wait_recv()

        @pl.when(first | (c > n))
        def _():
            @pl.loop(1, ng)
            def _(d):
                gather_copy(buf, n, d).start()

    def shared(buf, n):
        @pl.loop(1, ng)
        def _(d):
            s = lax.rem(g + d, ng)
            pltpu.make_async_remote_copy(
                src_ref=buf.at[s],
                dst_ref=buf.at[s],
                send_sem=ag_send.at[n, d],
                recv_sem=ag_recv.at[n, s],
                device_id={"gz": s},
                device_id_type=MESH,
            ).wait_recv()

    def column_copy(src, dst, n, d):
        return pltpu.make_async_remote_copy(
            src_ref=src,
            dst_ref=dst,
            send_sem=x_send.at[n, d],
            recv_sem=x_recv.at[n],
            device_id={"col": d},
            device_id_type=MESH,
        )

    for h in range(2):
        start = jnp.where(first, h * bs + g * ch, g * rows + h * ch)
        total = part[pl.ds(pl.multiple_of(start, ch), ch), :]

        def add(d, total):
            s = lax.rem(g + d, ng)
            pltpu.make_async_remote_copy(
                src_ref=land.at[h, s],
                dst_ref=land.at[h, s],
                send_sem=rs_send.at[h, s],
                recv_sem=rs_recv.at[h, s],
                device_id={"gz": s},
                device_id_type=MESH,
            ).wait_recv()
            return total + land[h, s]

        total = lax.fori_loop(1, ng, add, total)
        own[h * ch : (h + 1) * ch, :] = total
        if h == 0:

            @pl.when(first)
            def _():
                f0[g] = own[:ch, :]
                share(f0, 0)

    @pl.when(c == 0)
    def _():
        x0[...] = own[...]

        @pl.loop(1, nc)
        def _(d):
            column_copy(x0, x0, 0, d).start()

    @pl.when(jnp.logical_not(first))
    def _():
        share(f0, 0)

    @pl.when(c > 0)
    def _():
        column_copy(x0, x0, 0, 1).wait_recv()

    left = dot3(x0[...], m_hi[0], m_lo[0])

    @pl.when(first | (c > 0))
    def _():
        shared(f0, 0)

    @pl.when(c == 0)
    def _():
        own[...] = left

    @pl.when(c > 0)
    def _():
        hi, lo = split(f0[...].reshape(bs, -1))
        own[...] = own[...] - dot3(left, hi, lo)

    @pl.when(first)
    def _():
        f1[g] = own[ch:, :]
        share(f1, 1)

    @pl.when(jnp.logical_not(first) & (c == 1))
    def _():
        @pl.loop(2, nc)
        def _(d):
            column_copy(own, x1, 1, d).start()

        out_ref[...] = dot3(own[...], m_hi[1], m_lo[1])

    @pl.when(jnp.logical_not(first) & (c == 0))
    def _():
        out_ref[...] = own[...]

    @pl.when(jnp.logical_not(first) & (c > 1))
    def _():
        share(f1, 1)
        column_copy(own, x1, 1, 1).wait_recv()
        lower = dot3(x1[...], m_hi[1], m_lo[1])
        shared(f1, 1)
        hi, lo = split(f1[...].reshape(bs, -1))
        out_ref[...] = own[...] - dot3(lower, hi, lo)

    @pl.when(first)
    def _():
        shared(f1, 1)

        def place(buf, p):
            @pl.loop(0, rows)
            def _(i):
                src = order_s[p, g % (ng // 2) * rows + i]
                out_ref[pl.ds(i, 1), :] = buf[src // ch, pl.ds(src % ch, 1), :]

        @pl.when(g < ng // 2)
        def _():
            place(f0, 0)

        @pl.when(g >= ng // 2)
        def _():
            place(f1, 1)

    for p in range(2):

        @pl.loop(0, ng)
        def _(i):
            dest, copy = rs_copy(p, i)

            @pl.when(dest != g)
            def _():
                copy.wait_send()

    for n, buf in enumerate((f0, f1)):

        @pl.when(first & (c > n))
        def _():
            @pl.loop(1, nr)
            def _(d):
                down_copy(buf, n, d).wait_send()

        @pl.when(first | (c > n))
        def _():
            @pl.loop(1, ng)
            def _(d):
                gather_copy(buf, n, d).wait_send()

    @pl.when(c == 0)
    def _():
        @pl.loop(1, nc)
        def _(d):
            column_copy(x0, x0, 0, d).wait_send()

    @pl.when(jnp.logical_not(first) & (c == 1))
    def _():
        @pl.loop(2, nc)
        def _(d):
            column_copy(own, x1, 1, d).wait_send()


def on_device(ng, nr, nc, lower_sub, upper_sub, block_mask, front_base, pivot_inverse, pivot_order):
    slab, width = lower_sub.shape[1:]
    rows, cols = front_base.shape
    bs = pivot_inverse.shape[1]
    assert slab == 2 * bs and cols == bs and rows * ng == slab and pivot_inverse.shape[0] == 2
    ch = rows // 2
    steps = 8
    depth = width // steps
    vmem = pl.BlockSpec(memory_space=pltpu.VMEM)
    smem = pl.BlockSpec(memory_space=pltpu.SMEM)
    anywhere = pl.BlockSpec(memory_space=pl.ANY)
    dma = pltpu.SemaphoreType.DMA
    return pl.pallas_call(
        functools.partial(kernel, ng, nr, nc, steps),
        out_shape=jax.ShapeDtypeStruct((rows, cols), F32),
        in_specs=[anywhere, anywhere, smem, vmem, vmem, vmem, smem],
        out_specs=vmem,
        scratch_shapes=[
            pltpu.VMEM((2, steps, bs, depth), BF16),
            pltpu.VMEM((steps, depth, cols), BF16),
            pltpu.VMEM((slab, cols), F32),
            pltpu.VMEM((2, ng, ch, cols), F32),
            pltpu.VMEM((rows, cols), F32),
            pltpu.VMEM((ng, ch, cols), F32),
            pltpu.VMEM((ng, ch, cols), F32),
            pltpu.VMEM((rows, bs), F32),
            pltpu.VMEM((rows, bs), F32),
            pltpu.VMEM((2, bs, bs), BF16),
            pltpu.VMEM((2, bs, bs), BF16),
            dma((2, steps)),
            dma((steps,)),
            dma((2, ng)),
            dma((2, ng)),
            dma((2, nr)),
            dma((2,)),
            dma((2, ng)),
            dma((2, ng)),
            dma((2, nc)),
            dma((2,)),
        ],
        compiler_params=pltpu.CompilerParams(
            collective_id=0, has_side_effects=True, vmem_limit_bytes=48 * 1024 * 1024
        ),
    )(lower_sub, upper_sub, block_mask, front_base, pivot_inverse, pivot_order, pivot_order)


def solution(mesh):
    placed = (
        P("gz", "row", None),
        P("gz", None, "col"),
        P("gz", "row", "col"),
        P(("row", "gz"), "col"),
        P(),
        P(),
    )
    shape = mesh.shape
    return jax.shard_map(
        functools.partial(on_device, shape["gz"], shape["row"], shape["col"]),
        mesh=mesh,
        in_specs=placed,
        out_specs=P(("row", "gz"), "col"),
        check_vma=False,
    )
```

time: 362 us -> 39.1 us (0.11); the launches traced: 357 us -> 38.8 us
  waiting for transfers between devices: 263 us -> 0 us
  blocking collectives: 60 us -> 0 us
  Pallas kernels: 0 us -> 32.7 us
  matrix products: 13.4 us -> 0 us
  between operations: 13.3 us -> 0.01 us
    psum x4 -> x0, waiting for transfers between devices: 220 us -> none  [spread_2(): return lax.psum(block, axis)]
    all_gather x2 -> x0, blocking collectives: 60 us -> none  [on_device(): column_rows = lax.all_gather(front, 'gz', axis=0, tiled=True)]
    reduce_scatter x1 -> x0, waiting for transfers between devices: 43 us -> none  [on_device(): lax.psum_scatter(jnp.dot(left_factor, right_factor, preferred_element_typ...]
    pallas_call x0 -> x1, Pallas kernels: none -> 32.7 us  [on_device(): pl.pallas_call(functools.partial(kernel, ng, nr, nc, steps), out_shape=ja...]
    dot_general x7 -> x0, matrix products: 13.4 us -> none  [the longest x1 7.75 us: on_device(): jnp.dot(left_factor, right_factor, preferred_element_type=jnp.float32)]
    unnamed x6 -> x10, local copies, waits for them, and re-layouts: 0.02 us -> 6.14 us
    gather x2 -> x0, local copies, waits for them, and re-layouts: 3.83 us -> none  [on_device(): permuted = jnp.take(pivot_block, pivot_order[panel], axis=0)]
  transfers between devices with their start and end apart: 5 -> 0, of which waited for: 5 -> 0; matrix products, arithmetic and copies ran while one was open for 0% -> 0% of each run, Pallas kernels for 0% -> 0%
where the time goes in v1:
time: 39.1 us; the launch traced here: 38.8 us
  Pallas kernels  32.7 us (84%)
  local copies, waits for them, and re-layouts  6.14 us (16%)
    pallas_call x1, Pallas kernels, on_device(): pl.pallas_call(functools.partial(kernel, ng, nr, nc, steps), out_shape=ja...  32.7 us
    unnamed x10, local copies, waits for them, and re-layouts  6.14 us

profile of v1, /device:TPU:68, one launch (start us, length us, event | category | flops | bytes accessed | tf_op | source)
XLA Modules:
  0.0 38.8 jit_solution(3380693884740470452)
XLA Ops:
  0.0 0.8 %copy.7.mask_ref = s32[1,4,2]{2,1,0:T(4,128)S(1)} copy(s32[1,4,2]{1,2,0:T(2,128)} %param.8) | data formatting | bytes 64 | tf_op args[2]
  0.8 0.0 copy-start
  0.8 2.2 %copy-done = bf16[1,8192,256]{2,1,0:T(8,128)(2,1)S(1)} copy-done((bf16[1,8192,256]{2,1,0:T(8,128)(2,1)S(1)}, bf16[1,8192,256]{2,1,0:T(8,128)(2,1)}, u32[]{:S(2)}) %copy-start) | copy-done | bytes 4194328
  3.0 0.0 copy-start.1
  3.0 1.0 %copy-done.1 = f32[2,256,256]{2,1,0:T(8,128)S(1)} copy-done((f32[2,256,256]{2,1,0:T(8,128)S(1)}, f32[2,256,256]{2,1,0:T(8,128)}, u32[]{:S(2)}) %copy-start.1) | copy-done | bytes 524312
  4.0 0.0 copy-start.2
  4.0 0.8 %copy-done.2 = f32[64,256]{1,0:T(8,128)S(1)} copy-done((f32[64,256]{1,0:T(8,128)S(1)}, f32[64,256]{1,0:T(8,128)}, u32[]{:S(2)}) %copy-start.2) | copy-done | bytes 65560
  4.8 0.0 copy-start.3
  4.8 0.7 %copy-done.3 = s32[2,256]{1,0:T(2,128)S(1)} copy-done((s32[2,256]{1,0:T(2,128)S(1)}, s32[2,256]{1,0:T(2,128)}, u32[]{:S(2)}) %copy-start.3) | copy-done | bytes 2072
  5.5 32.7 %shard_map.64 = f32[64,256]{1,0:T(8,128)S(1)} custom-call(bf16[1,512,8192]{2,1,0:T(8,128)(2,1)} %a_hbm.1, bf16[1,8192,256]{2,1,0:T(8,128)(2,1)S(1)} %copy-done, s32[1,4,2]{2,1,0:T(4,128)S(1)} %copy.7.mask_ref, f32[64,256]{1,0:T(8,128)S(1)} %copy-done.2, f32[2,256,256]{2,1,0:T(8,128)S(1)} %copy-done.1, s32[2,256]{1,0:T(2,128)S(1)} %copy-done.3, ...), custom_call_target="tpu_custom_call" | custom-call | tf_op jit(solution)/shard_map/pallas_call | solution.py:333
  38.2 0.6 %copy.9 = f32[64,256]{1,0:T(8,128)} copy(f32[64,256]{1,0:T(8,128)S(1)} %shard_map.64) | data formatting | bytes 131072
Async XLA Ops:
  0.8 2.2 %copy-start = (bf16[1,8192,256]{2,1,0:T(8,128)(2,1)S(1)}, bf16[1,8192,256]{2,1,0:T(8,128)(2,1)}, u32[]{:S(2)}) copy-start(bf16[1,8192,256]{2,1,0:T(8,128)(2,1)} %b_hbm.1) | copy-start | bytes 12582916
  3.0 1.0 %copy-start.1 = (f32[2,256,256]{2,1,0:T(8,128)S(1)}, f32[2,256,256]{2,1,0:T(8,128)}, u32[]{:S(2)}) copy-start(f32[2,256,256]{2,1,0:T(8,128)} %inv_ref.1) | copy-start | bytes 1572868
  4.0 0.8 %copy-start.2 = (f32[64,256]{1,0:T(8,128)S(1)}, f32[64,256]{1,0:T(8,128)}, u32[]{:S(2)}) copy-start(f32[64,256]{1,0:T(8,128)} %base_ref.1) | copy-start | bytes 196612
  4.8 0.7 %copy-start.3 = (s32[2,256]{1,0:T(2,128)S(1)}, s32[2,256]{1,0:T(2,128)}, u32[]{:S(2)}) copy-start(s32[2,256]{1,0:T(2,128)} %order_s.1) | copy-start | bytes 6148

commit v2 on v1

v2 whole, which is shorter than its diff:
```python
import functools

import jax
import jax.numpy as jnp
from jax import lax
from jax.experimental import pallas as pl
from jax.experimental.pallas import tpu as pltpu
from jax.sharding import PartitionSpec as P

F32 = jnp.float32
BF16 = jnp.bfloat16
VMEM = 63 * 1024 * 1024
MESH = pl.DeviceIdType.MESH


def split(x):
    hi = x.astype(BF16)
    return hi, (x - hi.astype(F32)).astype(BF16)


def dot(a, b):
    return jnp.dot(a, b, preferred_element_type=F32)


def dot3(x, w_hi, w_lo):
    hi, lo = x
    n = hi.shape[0]
    both = dot(jnp.concatenate([hi, lo], axis=0), w_hi)
    return both[:n] + (both[n:] + dot(hi, w_lo))


def kernel(
    ng, nr, nc, steps,
    a_hbm, b_hbm, mask_hbm, base_hbm, inv_hbm, order_hbm,
    out_ref,
    a_v, b_v, mask_ref, base_ref, inv_ref, order_v, order_s,
    part, land, own, raw, f0, f1, x0, x1, m_hi, m_lo,
    a_sem, b_sem, in_sem, rs_send, rs_recv,
    z_send, z_recv, ag_send, ag_recv, x_send, x_recv, s_send, s_recv,
):
    g, r, c = lax.axis_index("gz"), lax.axis_index("row"), lax.axis_index("col")
    bs = inv_ref.shape[1]
    rows = own.shape[0]
    ch = rows // 2
    depth = a_v.shape[1] // steps
    mb = bs // mask_ref.shape[1]
    first = r == 0
    core = lax.rem(c, 2)
    others = jnp.logical_not(first)
    swap = jnp.where(first & (c == 0), 1, 0)
    halves = [slice(j * bs // 2, (j + 1) * bs // 2) for j in range(2)]

    def a_copy(h, k):
        return pltpu.make_async_copy(
            a_hbm.at[0, pl.ds(pl.multiple_of(lax.rem(h + swap, 2) * bs, bs), bs), pl.ds(k * depth, depth)],
            a_v.at[pl.ds(h * bs, bs), pl.ds(k * depth, depth)],
            a_sem.at[h, k],
        )

    def b_copy(k):
        return pltpu.make_async_copy(b_hbm.at[0, pl.ds(k * depth, depth), :], b_v.at[pl.ds(k * depth, depth), :], b_sem.at[k])

    def small(n, src, dst):
        copy = pltpu.make_async_copy(src, dst, in_sem.at[n])
        copy.start()
        return copy

    early = [small(0, mask_hbm, mask_ref), small(1, base_hbm, base_ref)]
    for k in range(steps):
        a_copy(0, k).start()
        b_copy(k).start()
    for k in range(steps):
        a_copy(1, k).start()
    late = [small(2, order_hbm, order_v), small(3, inv_hbm, inv_ref), small(4, order_hbm, order_s)]

    barrier = pltpu.get_barrier_semaphore()

    def greet(axis, me, n):
        @pl.loop(1, n)
        def _(d):
            pl.semaphore_signal(barrier, inc=1, device_id={axis: lax.rem(me + d, n)}, device_id_type=MESH)

    greet("gz", g, ng)
    greet("row", r, nr)
    greet("col", c, nc)

    def rs_copy(p, i):
        half = lax.rem(p + swap, 2)
        q = half * ng + i
        dest = jnp.where(first, i, q // 2)
        h = jnp.where(first, half, lax.rem(q, 2))
        return dest, pltpu.make_async_remote_copy(
            src_ref=part.at[pl.ds(pl.multiple_of(p * bs + i * ch, ch), ch), :],
            dst_ref=land.at[h, g],
            send_sem=rs_send.at[p, i],
            recv_sem=rs_recv.at[h, g],
            device_id={"gz": dest},
            device_id_type=MESH,
        )

    for p in range(2):
        top = p * bs
        half = lax.rem(p + swap, 2)
        at_once = 1 + p
        for k in range(0, steps, at_once):
            for n in range(k, k + at_once):
                if p == 0:
                    b_copy(n).wait()
                a_copy(p, n).wait()
            along = slice(k * depth, (k + at_once) * depth)
            for low in range(top, top + bs, bs // 2):
                term = dot(a_v[low : low + bs // 2, along], b_v[along, :])
                if k == 0:
                    part[low : low + bs // 2, :] = term
                else:
                    part[low : low + bs // 2, :] += term
        if p == 0:
            for copy in early:
                copy.wait()
        for i in range(bs // mb):
            for j in range(bs // mb):
                at = (slice(top + i * mb, top + (i + 1) * mb), slice(j * mb, (j + 1) * mb))
                part[at] = part[at] * mask_ref[0, j, half * (bs // mb) + i].astype(F32)

        @pl.when(g // (ng // 2) == half)
        def _():
            mine = pl.ds(pl.multiple_of(top + lax.rem(g, ng // 2) * rows, rows), rows)
            part[mine, :] = part[mine, :] + base_ref[...]

        if p == 0:
            pl.semaphore_wait(barrier, ng + nr + nc - 3)

        @pl.loop(0, ng)
        def _(d):
            i = lax.rem(d + g, ng)
            dest, copy = rs_copy(p, i)

            @pl.when(dest != g)
            def _():
                copy.start()

    def finish():
        for wait in pending:
            wait()

    def rs_wait():
        for p in range(2):

            @pl.loop(0, ng)
            def _(i):
                dest, copy = rs_copy(p, i)

                @pl.when(dest != g)
                def _():
                    copy.wait_send()

    pending = [rs_wait]

    def gather_copy(buf, n, j, s, d):
        return pltpu.make_async_remote_copy(
            src_ref=buf.at[j, s],
            dst_ref=buf.at[j, s],
            send_sem=ag_send.at[n, j, d],
            recv_sem=ag_recv.at[n, j, s],
            device_id={"gz": lax.rem(g + d, ng)},
            device_id_type=MESH,
        )

    def down(m, act):
        ref = (f0.at[0, g], f0.at[1, g], raw, x0.at[pl.ds(rows, ch), :])[m]

        @pl.loop(1, nr)
        def _(d):
            act(
                pltpu.make_async_remote_copy(
                    src_ref=ref,
                    dst_ref=ref,
                    send_sem=z_send.at[m, d],
                    recv_sem=z_recv.at[m],
                    device_id={"row": d},
                    device_id_type=MESH,
                )
            )

    def downs(m, act):
        pl.when(first & (c == 0 if m == 3 else c > m // 2))(lambda: down(m, act))

    def arrived(m):
        ref = (f0.at[0, g], f0.at[1, g], raw, x0.at[pl.ds(rows, ch), :])[m]
        pltpu.make_async_remote_copy(
            src_ref=ref,
            dst_ref=ref,
            send_sem=z_send.at[m, 1],
            recv_sem=z_recv.at[m],
            device_id={"row": 0},
            device_id_type=MESH,
        ).wait_recv()

    def gather(buf, n, j, act):
        @pl.when(first | (c > n))
        def _():
            @pl.loop(1, ng)
            def _(d):
                reads = jnp.logical_not(first) | (lax.rem(g + d, ng) >= n * (ng // 2))

                @pl.when(reads)
                def _():
                    act(gather_copy(buf, n, j, g, d))

    def begin(copy):
        copy.start()

    def end(copy):
        copy.wait_send()

    def shared(buf, n, j):
        @pl.loop(1, ng)
        def _(d):
            gather_copy(buf, n, j, lax.rem(g + d, ng), d).wait_recv()

    def column_part(m, which=None):
        if m == 2:
            return x1 if which is None else x1.at[which]
        top, size = ((0, rows), (rows, ch))[m]
        if which is None:
            return x0.at[pl.ds(top, size), :]
        return x0.at[pl.ds(pl.multiple_of(top + which * (size // 2), size // 2), size // 2), :]

    def column_copy(m, d, which=None):
        ref = column_part(m, which)
        return pltpu.make_async_remote_copy(
            src_ref=ref,
            dst_ref=ref,
            send_sem=x_send.at[m, d],
            recv_sem=x_recv.at[m],
            device_id={"col": d},
            device_id_type=MESH,
        )

    def sibling_copy(m, which):
        ref = column_part(m, which)
        return pltpu.make_async_remote_copy(
            src_ref=ref,
            dst_ref=ref,
            send_sem=s_send.at[m],
            recv_sem=s_recv.at[m],
            device_id={"col": c + 1 - 2 * core},
            device_id_type=MESH,
        )

    def columns(m, act, only=None):
        @pl.when(c == 0 if m == 1 else others & (c == m // 2))
        def _():
            if m < 2:
                pl.when(first if m == 1 else others)(lambda: act(column_copy(m, 1)))

            @pl.loop(2, nc)
            def _(d):
                if only is None:
                    act(column_copy(m, d, lax.rem(d, 2)))
                else:
                    pl.when(lax.rem(d, 2) == only)(lambda: act(column_copy(m, d, only)))

    def pass_on(m):
        column_copy(m, 1, core).wait_recv()
        sibling_copy(m, core).start()

    def passed_on(m):
        sibling_copy(m, 1 - core).wait_recv()

    for copy in late:
        copy.wait()

    for p in range(2):
        placer = (lax.broadcasted_iota(jnp.int32, (bs, bs), 0) == order_v[p : p + 1, :]).astype(BF16)
        for plain, ref in zip(split(inv_ref[p]), (m_hi, m_lo)):
            moved = lax.dot_general(plain, placer, (((1,), (1,)), ((), ())), preferred_element_type=F32)
            ref[p] = jnp.where(c == p, plain.astype(F32), moved).astype(BF16)

    for n in range(2):
        h = lax.rem(n + swap, 2)
        start = jnp.where(first, n * bs + g * ch, g * rows + n * ch)
        total = part[pl.ds(pl.multiple_of(start, ch), ch), :]

        def add(d, total):
            s = lax.rem(g + d, ng)
            pltpu.make_async_remote_copy(
                src_ref=land.at[h, s],
                dst_ref=land.at[h, s],
                send_sem=rs_send.at[n, s],
                recv_sem=rs_recv.at[h, s],
                device_id={"gz": s},
                device_id_type=MESH,
            ).wait_recv()
            return total + land[h, s]

        total = lax.fori_loop(1, ng, add, total)
        own[pl.ds(pl.multiple_of(h * ch, ch), ch), :] = total

        def panel_0_rows():
            for j, cols in enumerate(halves):
                f0[j, g] = own[:ch, cols]

        def panel_1_rows():
            raw[...] = own[ch:, :]

        if n == 0:

            @pl.when(first & (c == 0))
            def _():
                x0[:rows, :] = jnp.zeros((rows, bs), F32)
                x0[rows:, :] = own[ch:, :]
                columns(1, begin)

            pl.when(first & (c > 0))(panel_0_rows)
            for m in (3, 0, 1):
                downs(m, begin)
        else:
            pl.when(first & (c > 0))(panel_1_rows)
            pl.when(first & (c == 0))(panel_0_rows)
            downs(2, begin)

            @pl.when(first)
            def _():
                for j in range(2):
                    gather(f0, 0, j, begin)

    @pl.when(others & (c == 0))
    def _():
        x0[:rows, :] = own[...]
        columns(0, begin)
        arrived(3)
        columns(1, begin)

    @pl.when(others & (c > 0))
    def _():
        for j in range(2):
            arrived(j)
            gather(f0, 0, j, begin)

    @pl.when(others & (c == 1))
    def _():
        column_copy(0, 1).wait_recv()

    @pl.when(first & (c == 1))
    def _():
        column_copy(1, 1).wait_recv()

    @pl.when(others & (c > 1))
    def _():
        pass_on(0)

    @pl.when(c > 1)
    def _():
        pass_on(1)
        passed_on(1)

    @pl.when(others & (c > 1))
    def _():
        passed_on(0)

    left = dot3(split(x0[...]), m_hi[0], m_lo[0])
    left_parts = split(left)

    @pl.when(others & (c > 1))
    def _():
        arrived(2)

    for j, cols in enumerate(halves):

        @pl.when(first | (c > 0))
        def _():
            shared(f0, 0, j)

        @pl.when(c == 0)
        def _():
            own[:, cols] = left[:rows, cols]
            f1[j, g] = left[rows:, cols]

        @pl.when(c > 0)
        def _():
            update = dot3(left_parts, *split(f0[j].reshape(bs, -1)))
            f1[j, g] = raw[:, cols] - update[rows:]
            own[:, cols] = own[:, cols] - update[:rows]

        gather(f1, 1, j, begin)

        @pl.when(others & (c == 1))
        def _():
            x1[j] = own[:, cols]

        columns(2, begin, j)

    def all_sent():
        for m in range(4):
            downs(m, end)
        for m in range(3):
            columns(m, end)

            @pl.when((others | (m == 1)) & (c > 1))
            def _():
                sibling_copy(m, core).wait_send()

        for n, buf in enumerate((f0, f1)):
            for j in range(2):
                gather(buf, n, j, end)

    pending.append(all_sent)

    @pl.when(others & (c == 1))
    def _():
        out_ref[...] = dot3(split(own[...]), m_hi[1], m_lo[1])

    @pl.when(others & (c == 0))
    def _():
        out_ref[...] = own[...]

    @pl.when(others & (c > 1))
    def _():
        pass_on(2)
        passed_on(2)
        lower = 0.0
        for j, cols in enumerate(halves):
            lower = lower + dot3(split(x1[j]), m_hi[1, cols, :], m_lo[1, cols, :])
        lower_parts = split(lower)
        for j, cols in enumerate(halves):
            shared(f1, 1, j)
            out_ref[:, cols] = own[:, cols] - dot3(lower_parts, *split(f1[j].reshape(bs, -1)))

    @pl.when(first)
    def _():
        def place(buf, p):
            @pl.loop(0, rows)
            def _(i):
                src = order_s[p, g % (ng // 2) * rows + i]
                row = [buf[j, src // ch, pl.ds(src % ch, 1), :] for j in range(2)]
                out_ref[pl.ds(i, 1), :] = jnp.concatenate(row, axis=1)

        @pl.when(g < ng // 2)
        def _():
            place(f0, 0)

        @pl.when(g >= ng // 2)
        def _():
            for j in range(2):
                shared(f1, 1, j)
            place(f1, 1)

    finish()


def on_device(ng, nr, nc, lower_sub, upper_sub, block_mask, front_base, pivot_inverse, pivot_order):
    slab, width = lower_sub.shape[1:]
    rows, cols = front_base.shape
    bs = pivot_inverse.shape[1]
    assert slab == 2 * bs and cols == bs and rows * ng == slab and pivot_inverse.shape[0] == 2
    ch = rows // 2
    steps = 8
    tiles = jnp.swapaxes(block_mask, 1, 2)
    vmem = pl.BlockSpec(memory_space=pltpu.VMEM)
    hbm = pl.BlockSpec(memory_space=pltpu.HBM)
    dma = pltpu.SemaphoreType.DMA
    return pl.pallas_call(
        functools.partial(kernel, ng, nr, nc, steps),
        out_shape=jax.ShapeDtypeStruct((rows, cols), F32),
        in_specs=[hbm] * 6,
        out_specs=vmem,
        scratch_shapes=[
            pltpu.VMEM((slab, width), BF16),
            pltpu.VMEM((width, cols), BF16),
            pltpu.SMEM(tiles.shape, jnp.int32),
            pltpu.VMEM((rows, cols), F32),
            pltpu.VMEM(pivot_inverse.shape, F32),
            pltpu.VMEM(pivot_order.shape, jnp.int32),
            pltpu.SMEM(pivot_order.shape, jnp.int32),
            pltpu.VMEM((slab, cols), F32),
            pltpu.VMEM((2, ng, ch, cols), F32),
            pltpu.VMEM((rows, cols), F32),
            pltpu.VMEM((ch, cols), F32),
            pltpu.VMEM((2, ng, ch, cols // 2), F32),
            pltpu.VMEM((2, ng, ch, cols // 2), F32),
            pltpu.VMEM((rows + ch, bs), F32),
            pltpu.VMEM((2, rows, bs // 2), F32),
            pltpu.VMEM((2, bs, bs), BF16),
            pltpu.VMEM((2, bs, bs), BF16),
            dma((2, steps)),
            dma((steps,)),
            dma((5,)),
            dma((2, ng)),
            dma((2, ng)),
            dma((4, nr)),
            dma((4,)),
            dma((2, 2, ng)),
            dma((2, 2, ng)),
            dma((3, nc)),
            dma((3,)),
            dma((3,)),
            dma((3,)),
        ],
        compiler_params=pltpu.CompilerParams(
            collective_id=0, has_side_effects=True, vmem_limit_bytes=VMEM
        ),
    )(lower_sub, upper_sub, tiles, front_base, pivot_inverse, pivot_order)


def solution(mesh):
    placed = (
        P("gz", "row", None),
        P("gz", None, "col"),
        P("gz", "row", "col"),
        P(("row", "gz"), "col"),
        P(),
        P(),
    )
    shape = mesh.shape
    return jax.shard_map(
        functools.partial(on_device, shape["gz"], shape["row"], shape["col"]),
        mesh=mesh,
        in_specs=placed,
        out_specs=P(("row", "gz"), "col"),
        check_vma=False,
    )
```

time: 39.1 us -> 31.7 us (0.81)
  local copies, waits for them, and re-layouts: 6.14 us -> 1.47 us
  Pallas kernels: 32.7 us -> 29.9 us
    unnamed x10 -> x1, local copies, waits for them, and re-layouts: 6.14 us -> 1.47 us
    pallas_call x1, Pallas kernels: 32.7 us -> 29.9 us  [on_device(): pl.pallas_call(functools.partial(kernel, ng, nr, nc, steps), out_shape=ja...]
where the time goes in v2:
time: 31.7 us; the launch traced here: 31.4 us
  Pallas kernels  29.9 us (94%)
  local copies, waits for them, and re-layouts  1.47 us (5%)
    pallas_call x1, Pallas kernels, on_device(): pl.pallas_call(functools.partial(kernel, ng, nr, nc, steps), out_shape=ja...  29.9 us
    unnamed x1, local copies, waits for them, and re-layouts  1.47 us

profile of v2, /device:TPU:68, one launch (start us, length us, event | category | flops | bytes accessed | tf_op | source)
XLA Modules:
  0.0 31.4 jit_solution(3257176499224720575)
XLA Ops:
  0.0 29.9 %shard_map.64 = f32[64,256]{1,0:T(8,128)} custom-call(bf16[1,512,8192]{2,1,0:T(8,128)(2,1)} %a_hbm.1, bf16[1,8192,256]{2,1,0:T(8,128)(2,1)} %b_hbm.1, s32[1,2,4]{2,1,0:T(2,128)} %bitcast.1, f32[64,256]{1,0:T(8,128)} %base_hbm.1, f32[2,256,256]{2,1,0:T(8,128)} %inv_hbm.1, s32[2,256]{1,0:T(2,128)} %order_hbm.1), custom_call_target="tpu_custom_call" | custom-call | tf_op jit(solution)/shard_map/pallas_call | solution.py:463
  29.9 1.5 %copy.8 = f32[64,256]{1,0:T(8,128)} copy(f32[64,256]{1,0:T(8,128)} %shard_map.64) | data formatting | bytes 131072

commit v3 on v2

--- a/solution.py
+++ b/solution.py
@@ -84,6 +84,19 @@
     greet("row", r, nr)
     greet("col", c, nc)
 
+    def landed(ref, sem):
+        pltpu.make_async_remote_copy(
+            src_ref=ref, dst_ref=ref, send_sem=sem, recv_sem=sem, device_id={"gz": g}, device_id_type=MESH
+        ).wait_recv()
+
+    def sent(ref, sem):
+        pltpu.make_async_remote_copy(
+            src_ref=ref, dst_ref=ref, send_sem=sem, recv_sem=sem, device_id={"gz": g}, device_id_type=MESH
+        ).wait_send()
+
+    def strips(n):
+        return part.at[pl.ds(0, n * ch), :]
+
     def rs_copy(p, i):
         half = lax.rem(p + swap, 2)
         q = half * ng + i
@@ -92,8 +105,8 @@
         return dest, pltpu.make_async_remote_copy(
             src_ref=part.at[pl.ds(pl.multiple_of(p * bs + i * ch, ch), ch), :],
             dst_ref=land.at[h, g],
-            send_sem=rs_send.at[p, i],
-            recv_sem=rs_recv.at[h, g],
+            send_sem=rs_send,
+            recv_sem=rs_recv.at[h],
             device_id={"gz": dest},
             device_id_type=MESH,
         )
@@ -101,7 +114,7 @@
     for p in range(2):
         top = p * bs
         half = lax.rem(p + swap, 2)
-        at_once = 1 + p
+        at_once = (1, steps // 2)[p]
         for k in range(0, steps, at_once):
             for n in range(k, k + at_once):
                 if p == 0:
@@ -139,99 +152,85 @@
             def _():
                 copy.start()
 
-    def finish():
-        for wait in pending:
-            wait()
-
-    def rs_wait():
-        for p in range(2):
-
-            @pl.loop(0, ng)
-            def _(i):
-                dest, copy = rs_copy(p, i)
-
-                @pl.when(dest != g)
-                def _():
-                    copy.wait_send()
-
-    pending = [rs_wait]
-
-    def gather_copy(buf, n, j, s, d):
+    def gather_copy(buf, n, j, d):
         return pltpu.make_async_remote_copy(
-            src_ref=buf.at[j, s],
-            dst_ref=buf.at[j, s],
-            send_sem=ag_send.at[n, j, d],
-            recv_sem=ag_recv.at[n, j, s],
+            src_ref=buf.at[j, g],
+            dst_ref=buf.at[j, g],
+            send_sem=ag_send.at[n, j],
+            recv_sem=ag_recv.at[n, j],
             device_id={"gz": lax.rem(g + d, ng)},
             device_id_type=MESH,
         )
 
-    def down(m, act):
-        ref = (f0.at[0, g], f0.at[1, g], raw, x0.at[pl.ds(rows, ch), :])[m]
-
-        @pl.loop(1, nr)
-        def _(d):
-            act(
-                pltpu.make_async_remote_copy(
-                    src_ref=ref,
-                    dst_ref=ref,
-                    send_sem=z_send.at[m, d],
-                    recv_sem=z_recv.at[m],
-                    device_id={"row": d},
-                    device_id_type=MESH,
-                )
-            )
-
-    def downs(m, act):
-        pl.when(first & (c == 0 if m == 3 else c > m // 2))(lambda: down(m, act))
+    def down_ref(m):
+        return (f0.at[0, g], f0.at[1, g], raw.at[0], raw.at[1], x0.at[pl.ds(rows, ch), :])[m]
+
+    def down_copy(m, d):
+        return pltpu.make_async_remote_copy(
+            src_ref=down_ref(m),
+            dst_ref=down_ref(m),
+            send_sem=z_send.at[m],
+            recv_sem=z_recv.at[m],
+            device_id={"row": d},
+            device_id_type=MESH,
+        )
+
+    def down(m):
+        @pl.when(first & (c == 0 if m == 4 else c > m // 2))
+        def _():
+            @pl.loop(1, nr)
+            def _(d):
+                down_copy(m, d).start()
+
+    def down_end(m):
+        @pl.when(first & (c == 0 if m == 4 else c > m // 2))
+        def _():
+            sent(strips(nr - 1) if m == 4 else f0.at[0, pl.ds(0, nr - 1)], z_send.at[m])
 
     def arrived(m):
-        ref = (f0.at[0, g], f0.at[1, g], raw, x0.at[pl.ds(rows, ch), :])[m]
-        pltpu.make_async_remote_copy(
-            src_ref=ref,
-            dst_ref=ref,
-            send_sem=z_send.at[m, 1],
-            recv_sem=z_recv.at[m],
-            device_id={"row": 0},
-            device_id_type=MESH,
-        ).wait_recv()
-
-    def gather(buf, n, j, act):
+        down_copy(m, 0).wait_recv()
+
+    def gather(buf, n, j):
         @pl.when(first | (c > n))
         def _():
             @pl.loop(1, ng)
             def _(d):
-                reads = jnp.logical_not(first) | (lax.rem(g + d, ng) >= n * (ng // 2))
+                reads = others | (lax.rem(g + d, ng) >= n * (ng // 2))
 
                 @pl.when(reads)
                 def _():
-                    act(gather_copy(buf, n, j, g, d))
-
-    def begin(copy):
-        copy.start()
-
-    def end(copy):
-        copy.wait_send()
+                    gather_copy(buf, n, j, d).start()
+
+    def gather_end(buf, n, j):
+        def ended(count):
+            sent(buf.at[j, pl.ds(0, count)], ag_send.at[n, j])
+
+        if n == 0:
+            pl.when(first | (c > n))(lambda: ended(ng - 1))
+        else:
+            pl.when(others & (c > n))(lambda: ended(ng - 1))
+            pl.when(first & (g < ng // 2))(lambda: ended(ng // 2))
+            if ng > 2:
+                pl.when(first & (g >= ng // 2))(lambda: ended(ng // 2 - 1))
 
     def shared(buf, n, j):
-        @pl.loop(1, ng)
-        def _(d):
-            gather_copy(buf, n, j, lax.rem(g + d, ng), d).wait_recv()
+        landed(buf.at[j, pl.ds(0, ng - 1)], ag_recv.at[n, j])
 
     def column_part(m, which=None):
+        if m == 1:
+            return x0.at[pl.ds(rows, ch), :]
         if m == 2:
-            return x1 if which is None else x1.at[which]
-        top, size = ((0, rows), (rows, ch))[m]
+            return x1.at[which]
         if which is None:
-            return x0.at[pl.ds(top, size), :]
-        return x0.at[pl.ds(pl.multiple_of(top + which * (size // 2), size // 2), size // 2), :]
+            return x0.at[pl.ds(0, rows), :]
+        return x0.at[pl.ds(pl.multiple_of(which * ch, ch), ch), :]
 
     def column_copy(m, d, which=None):
         ref = column_part(m, which)
         return pltpu.make_async_remote_copy(
             src_ref=ref,
             dst_ref=ref,
-            send_sem=x_send.at[m, d],
+            send_sem=x_send.at[m],
             recv_sem=x_recv.at[m],
             device_id={"col": d},
             device_id_type=MESH,
@@ -248,18 +247,25 @@
             device_id_type=MESH,
         )
 
-    def columns(m, act, only=None):
+    def columns(m, only=None):
         @pl.when(c == 0 if m == 1 else others & (c == m // 2))
         def _():
-            if m < 2:
-                pl.when(first if m == 1 else others)(lambda: act(column_copy(m, 1)))
-
-            @pl.loop(2, nc)
+            @pl.loop(1 if m == 1 else 2, nc)
             def _(d):
-                if only is None:
-                    act(column_copy(m, d, lax.rem(d, 2)))
+                if m == 1:
+                    pl.when(first | (d > 1))(lambda: column_copy(m, d).start())
+                elif only is None:
+                    column_copy(m, d, lax.rem(d, 2)).start()
                 else:
-                    pl.when(lax.rem(d, 2) == only)(lambda: act(column_copy(m, d, only)))
+                    pl.when(lax.rem(d, 2) == only)(lambda: column_copy(m, d, only).start())
+
+    def columns_end(m):
+        if m == 1:
+            pl.when(first & (c == 0))(lambda: sent(strips(nc - 1), x_send.at[m]))
+            pl.when(others & (c == 0))(lambda: sent(strips(nc - 2), x_send.at[m]))
+        else:
+            count = nc if m == 0 else nc - 2
+            pl.when(others & (c == m // 2))(lambda: sent(strips(count), x_send.at[m]))
 
     def pass_on(m):
         column_copy(m, 1, core).wait_recv()
@@ -280,21 +286,11 @@
     for n in range(2):
         h = lax.rem(n + swap, 2)
         start = jnp.where(first, n * bs + g * ch, g * rows + n * ch)
-        total = part[pl.ds(pl.multiple_of(start, ch), ch), :]
-
-        def add(d, total):
-            s = lax.rem(g + d, ng)
-            pltpu.make_async_remote_copy(
-                src_ref=land.at[h, s],
-                dst_ref=land.at[h, s],
-                send_sem=rs_send.at[n, s],
-                recv_sem=rs_recv.at[h, s],
-                device_id={"gz": s},
-                device_id_type=MESH,
-            ).wait_recv()
-            return total + land[h, s]
-
-        total = lax.fori_loop(1, ng, add, total)
+        landed(land.at[h, pl.ds(0, ng - 1)], rs_recv.at[h])
+        land[h, g] = part[pl.ds(pl.multiple_of(start, ch), ch), :]
+        total = land[h, 0]
+        for m in range(1, ng):
+            total = total + land[h, m]
         own[pl.ds(pl.multiple_of(h * ch, ch), ch), :] = total
 
         def panel_0_rows():
@@ -302,110 +298,112 @@
                 f0[j, g] = own[:ch, cols]
 
         def panel_1_rows():
-            raw[...] = own[ch:, :]
+            for j, cols in enumerate(halves):
+                raw[j] = own[ch:, cols]
 
         if n == 0:
 
             @pl.when(first & (c == 0))
             def _():
-                x0[:rows, :] = jnp.zeros((rows, bs), F32)
                 x0[rows:, :] = own[ch:, :]
-                columns(1, begin)
+                columns(1)
 
             pl.when(first & (c > 0))(panel_0_rows)
-            for m in (3, 0, 1):
-                downs(m, begin)
+            for m in (4, 0, 1):
+                down(m)
         else:
             pl.when(first & (c > 0))(panel_1_rows)
             pl.when(first & (c == 0))(panel_0_rows)
-            downs(2, begin)
+            down(2)
+            down(3)
 
             @pl.when(first)
             def _():
                 for j in range(2):
-                    gather(f0, 0, j, begin)
+                    gather(f0, 0, j)
 
     @pl.when(others & (c == 0))
     def _():
         x0[:rows, :] = own[...]
-        columns(0, begin)
-        arrived(3)
-        columns(1, begin)
+        column_copy(0, 1).start()
+        arrived(4)
+        columns(1)
+        columns(0)
 
     @pl.when(others & (c > 0))
     def _():
         for j in range(2):
             arrived(j)
-            gather(f0, 0, j, begin)
-
-    @pl.when(others & (c == 1))
-    def _():
-        column_copy(0, 1).wait_recv()
-
-    @pl.when(first & (c == 1))
-    def _():
-        column_copy(1, 1).wait_recv()
-
-    @pl.when(others & (c > 1))
-    def _():
-        pass_on(0)
-
-    @pl.when(c > 1)
-    def _():
-        pass_on(1)
-        passed_on(1)
-
-    @pl.when(others & (c > 1))
-    def _():
-        passed_on(0)
-
-    left = dot3(split(x0[...]), m_hi[0], m_lo[0])
-    left_parts = split(left)
-
-    @pl.when(others & (c > 1))
-    def _():
-        arrived(2)
-
-    for j, cols in enumerate(halves):
-
-        @pl.when(first | (c > 0))
-        def _():
+            gather(f0, 0, j)
+
+    @pl.when(first | (c > 1))
+    def _():
+        @pl.when(c > 0)
+        def _():
+            column_copy(1, 1).wait_recv()
+
+        lower = dot3(split(x0[rows:, :]), m_hi[0], m_lo[0])
+        parts = split(lower)
+
+        for j, cols in enumerate(halves):
+
+            @pl.when(others)
+            def _():
+                arrived(2 + j)
+
             shared(f0, 0, j)
 
+            @pl.when(c == 0)
+            def _():
+                f1[j, g] = lower[:, cols]
+
+            @pl.when(c > 0)
+            def _():
+                f1[j, g] = raw[j] - dot3(parts, *split(f0[j].reshape(bs, -1)))
+
+            gather(f1, 1, j)
+
+    @pl.when(others)
+    def _():
+        @pl.when(c == 1)
+        def _():
+            column_copy(0, 1).wait_recv()
+
+        @pl.when(c > 1)
+        def _():
+            pass_on(0)
+            passed_on(0)
+
+        lower = dot3(split(x0[:rows, :]), m_hi[0], m_lo[0])
+        parts = split(lower)
+
         @pl.when(c == 0)
         def _():
-            own[:, cols] = left[:rows, cols]
-            f1[j, g] = left[rows:, cols]
+            own[...] = lower
 
         @pl.when(c > 0)
         def _():
-            update = dot3(left_parts, *split(f0[j].reshape(bs, -1)))
-            f1[j, g] = raw[:, cols] - update[rows:]
-            own[:, cols] = own[:, cols] - update[:rows]
-
-        gather(f1, 1, j, begin)
-
-        @pl.when(others & (c == 1))
-        def _():
-            x1[j] = own[:, cols]
-
-        columns(2, begin, j)
-
-    def all_sent():
-        for m in range(4):
-            downs(m, end)
-        for m in range(3):
-            columns(m, end)
-
-            @pl.when((others | (m == 1)) & (c > 1))
-            def _():
-                sibling_copy(m, core).wait_send()
-
-        for n, buf in enumerate((f0, f1)):
-            for j in range(2):
-                gather(buf, n, j, end)
-
-    pending.append(all_sent)
+            for j, cols in enumerate(halves):
+
+                @pl.when(c == 1)
+                def _():
+                    shared(f0, 0, j)
+
+                own[:, cols] = own[:, cols] - dot3(parts, *split(f0[j].reshape(bs, -1)))
+
+                @pl.when(c == 1)
+                def _():
+                    x1[j] = own[:, cols]
+                    columns(2, j)
+
+    sent(strips(2 * (ng - 1)), rs_send)
+    for m in range(5):
+        down_end(m)
+    for m in range(2):
+        columns_end(m)
+    for j in range(2):
+        gather_end(f0, 0, j)
+    pl.when(others & (c > 1))(lambda: sibling_copy(0, core).wait_send())
 
     @pl.when(others & (c == 1))
     def _():
@@ -430,7 +428,7 @@
     @pl.when(first)
     def _():
         def place(buf, p):
-            @pl.loop(0, rows)
+            @pl.loop(0, rows, unroll=8)
             def _(i):
                 src = order_s[p, g % (ng // 2) * rows + i]
                 row = [buf[j, src // ch, pl.ds(src % ch, 1), :] for j in range(2)]
@@ -446,7 +444,10 @@
                 shared(f1, 1, j)
             place(f1, 1)
 
-    finish()
+    columns_end(2)
+    for j in range(2):
+        gather_end(f1, 1, j)
+    pl.when(others & (c > 1))(lambda: sibling_copy(2, core).wait_send())
 
 
 def on_device(ng, nr, nc, lower_sub, upper_sub, block_mask, front_base, pivot_inverse, pivot_order):
@@ -476,7 +477,7 @@
             pltpu.VMEM((slab, cols), F32),
             pltpu.VMEM((2, ng, ch, cols), F32),
             pltpu.VMEM((rows, cols), F32),
-            pltpu.VMEM((ch, cols), F32),
+            pltpu.VMEM((2, ch, cols // 2), F32),
             pltpu.VMEM((2, ng, ch, cols // 2), F32),
             pltpu.VMEM((2, ng, ch, cols // 2), F32),
             pltpu.VMEM((rows + ch, bs), F32),
@@ -486,13 +487,13 @@
             dma((2, steps)),
             dma((steps,)),
             dma((5,)),
-            dma((2, ng)),
-            dma((2, ng)),
-            dma((4, nr)),
-            dma((4,)),
-            dma((2, 2, ng)),
-            dma((2, 2, ng)),
-            dma((3, nc)),
+            dma(()),
+            dma((2,)),
+            dma((5,)),
+            dma((5,)),
+            dma((2, 2)),
+            dma((2, 2)),
+            dma((3,)),
             dma((3,)),
             dma((3,)),
             dma((3,)),

time: 31.7 us -> 30 us (0.946)
  Pallas kernels: 29.9 us -> 28.3 us
    pallas_call x1, Pallas kernels: 29.9 us -> 28.3 us  [on_device(): pl.pallas_call(functools.partial(kernel, ng, nr, nc, steps), out_shape=ja...]
where the time goes in v3:
time: 30 us; the launch traced here: 29.8 us
  Pallas kernels  28.3 us (94%)
  local copies, waits for them, and re-layouts  1.47 us (5%)
    pallas_call x1, Pallas kernels, on_device(): pl.pallas_call(functools.partial(kernel, ng, nr, nc, steps), out_shape=ja...  28.3 us
    unnamed x1, local copies, waits for them, and re-layouts  1.47 us

profile of v3, /device:TPU:68, one launch (start us, length us, event | category | flops | bytes accessed | tf_op | source)
XLA Modules:
  0.0 29.8 jit_solution(12491781501828858813)
XLA Ops:
  0.0 28.3 %shard_map.64 = f32[64,256]{1,0:T(8,128)} custom-call(bf16[1,512,8192]{2,1,0:T(8,128)(2,1)} %a_hbm.1, bf16[1,8192,256]{2,1,0:T(8,128)(2,1)} %b_hbm.1, s32[1,2,4]{2,1,0:T(2,128)} %bitcast.1, f32[64,256]{1,0:T(8,128)} %base_hbm.1, f32[2,256,256]{2,1,0:T(8,128)} %inv_hbm.1, s32[2,256]{1,0:T(2,128)} %order_hbm.1), custom_call_target="tpu_custom_call" | custom-call | tf_op jit(solution)/shard_map/pallas_call | solution.py:464
  28.3 1.5 %copy.8 = f32[64,256]{1,0:T(8,128)} copy(f32[64,256]{1,0:T(8,128)} %shard_map.64) | data formatting | bytes 131072

commit v4 on v3

--- a/solution.py
+++ b/solution.py
@@ -9,7 +9,7 @@
 
 F32 = jnp.float32
 BF16 = jnp.bfloat16
-VMEM = 63 * 1024 * 1024
+VMEM = 48 * 1024 * 1024
 MESH = pl.DeviceIdType.MESH
 
 
@@ -114,7 +114,7 @@
     for p in range(2):
         top = p * bs
         half = lax.rem(p + swap, 2)
-        at_once = (1, steps // 2)[p]
+        at_once = (1, 2)[p]
         for k in range(0, steps, at_once):
             for n in range(k, k + at_once):
                 if p == 0:
@@ -456,8 +456,9 @@
     bs = pivot_inverse.shape[1]
     assert slab == 2 * bs and cols == bs and rows * ng == slab and pivot_inverse.shape[0] == 2
     ch = rows // 2
-    steps = 8
+    steps = 4
     tiles = jnp.swapaxes(block_mask, 1, 2)
+    operands = (lower_sub, upper_sub, tiles, front_base, pivot_inverse, pivot_order)
     vmem = pl.BlockSpec(memory_space=pltpu.VMEM)
     hbm = pl.BlockSpec(memory_space=pltpu.HBM)
     dma = pltpu.SemaphoreType.DMA
@@ -501,7 +502,7 @@
         compiler_params=pltpu.CompilerParams(
             collective_id=0, has_side_effects=True, vmem_limit_bytes=VMEM
         ),
-    )(lower_sub, upper_sub, tiles, front_base, pivot_inverse, pivot_order)
+    )(*[pltpu.with_memory_space_constraint(x, pltpu.HBM) for x in operands])
 
 
 def solution(mesh):

time: 30 us -> 28.3 us (0.943)
  local copies, waits for them, and re-layouts: 1.47 us -> 0.63 us
  Pallas kernels: 28.3 us -> 27.5 us
    unnamed x1, local copies, waits for them, and re-layouts: 1.47 us -> 0.63 us
    pallas_call x1, Pallas kernels: 28.3 us -> 27.5 us  [on_device(): pl.pallas_call(functools.partial(kernel, ng, nr, nc, steps), out_shape=ja...]
where the time goes in v4:
time: 28.3 us; the launch traced here: 28.2 us
  Pallas kernels  27.5 us (97%)
  local copies, waits for them, and re-layouts  0.63 us (2%)
    pallas_call x1, Pallas kernels, on_device(): pl.pallas_call(functools.partial(kernel, ng, nr, nc, steps), out_shape=ja...  27.5 us
    unnamed x1, local copies, waits for them, and re-layouts  0.63 us

profile of v4, /device:TPU:68, one launch (start us, length us, event | category | flops | bytes accessed | tf_op | source)
XLA Modules:
  0.0 28.2 jit_solution(3580561011070916435)
XLA Ops:
  0.0 27.5 %shard_map.64 = f32[64,256]{1,0:T(8,128)S(1)} custom-call(bf16[1,512,8192]{2,1,0:T(8,128)(2,1)} %a_hbm.1, bf16[1,8192,256]{2,1,0:T(8,128)(2,1)} %b_hbm.1, s32[1,2,4]{2,1,0:T(2,128)} %bitcast.1, f32[64,256]{1,0:T(8,128)} %base_hbm.1, f32[2,256,256]{2,1,0:T(8,128)} %inv_hbm.1, s32[2,256]{1,0:T(2,128)} %order_hbm.1), custom_call_target="tpu_custom_call" | custom-call | tf_op jit(solution)/shard_map/pallas_call | solution.py:465
  27.5 0.6 %copy.8 = f32[64,256]{1,0:T(8,128)} copy(f32[64,256]{1,0:T(8,128)S(1)} %shard_map.64) | data formatting | bytes 131072

commit v5 on v4

--- a/solution.py
+++ b/solution.py
@@ -46,6 +46,7 @@
     mb = bs // mask_ref.shape[1]
     first = r == 0
     core = lax.rem(c, 2)
+    far_first = sorted(range(1, ng), key=lambda d: abs(2 * d - ng))
     others = jnp.logical_not(first)
     swap = jnp.where(first & (c == 0), 1, 0)
     halves = [slice(j * bs // 2, (j + 1) * bs // 2) for j in range(2)]
@@ -143,8 +144,7 @@
         if p == 0:
             pl.semaphore_wait(barrier, ng + nr + nc - 3)
 
-        @pl.loop(0, ng)
-        def _(d):
+        for d in far_first + [0]:
             i = lax.rem(d + g, ng)
             dest, copy = rs_copy(p, i)
 
@@ -193,8 +193,7 @@
     def gather(buf, n, j):
         @pl.when(first | (c > n))
         def _():
-            @pl.loop(1, ng)
-            def _(d):
+            for d in far_first:
                 reads = others | (lax.rem(g + d, ng) >= n * (ng // 2))
 
                 @pl.when(reads)
@@ -311,13 +310,18 @@
             pl.when(first & (c > 0))(panel_0_rows)
             for m in (4, 0, 1):
                 down(m)
+
+            @pl.when(first & (c > 0))
+            def _():
+                for j in range(2):
+                    gather(f0, 0, j)
         else:
             pl.when(first & (c > 0))(panel_1_rows)
             pl.when(first & (c == 0))(panel_0_rows)
             down(2)
             down(3)
 
-            @pl.when(first)
+            @pl.when(first & (c == 0))
             def _():
                 for j in range(2):
                     gather(f0, 0, j)

time: 28.3 us -> 28 us (0.989)
  Pallas kernels: 27.5 us -> 27.1 us
    pallas_call x1, Pallas kernels: 27.5 us -> 27.1 us  [on_device(): pl.pallas_call(functools.partial(kernel, ng, nr, nc, steps), out_shape=ja...]
where the time goes in v5:
time: 28 us; the launch traced here: 27.8 us
  Pallas kernels  27.1 us (97%)
  local copies, waits for them, and re-layouts  0.63 us (2%)
    pallas_call x1, Pallas kernels, on_device(): pl.pallas_call(functools.partial(kernel, ng, nr, nc, steps), out_shape=ja...  27.1 us
    unnamed x1, local copies, waits for them, and re-layouts  0.63 us

profile of v5, /device:TPU:68, one launch (start us, length us, event | category | flops | bytes accessed | tf_op | source)
XLA Modules:
  0.0 27.8 jit_solution(139441355237526157)
XLA Ops:
  0.0 27.1 %shard_map.64 = f32[64,256]{1,0:T(8,128)S(1)} custom-call(bf16[1,512,8192]{2,1,0:T(8,128)(2,1)} %a_hbm.1, bf16[1,8192,256]{2,1,0:T(8,128)(2,1)} %b_hbm.1, s32[1,2,4]{2,1,0:T(2,128)} %bitcast.1, f32[64,256]{1,0:T(8,128)} %base_hbm.1, f32[2,256,256]{2,1,0:T(8,128)} %inv_hbm.1, s32[2,256]{1,0:T(2,128)} %order_hbm.1), custom_call_target="tpu_custom_call" | custom-call | tf_op jit(solution)/shard_map/pallas_call | solution.py:469
  27.2 0.6 %copy.8 = f32[64,256]{1,0:T(8,128)} copy(f32[64,256]{1,0:T(8,128)S(1)} %shard_map.64) | data formatting | bytes 131072

commit v6 on v5

--- a/solution.py
+++ b/solution.py
@@ -66,6 +66,17 @@
         copy.start()
         return copy
 
+    barrier = pltpu.get_barrier_semaphore()
+
+    def greet(axis, me, n):
+        @pl.loop(1, n)
+        def _(d):
+            pl.semaphore_signal(barrier, inc=1, device_id={axis: lax.rem(me + d, n)}, device_id_type=MESH)
+
+    greet("row", r, nr)
+    greet("gz", g, ng)
+    greet("col", c, nc)
+
     early = [small(0, mask_hbm, mask_ref), small(1, base_hbm, base_ref)]
     for k in range(steps):
         a_copy(0, k).start()
@@ -73,17 +84,6 @@
     for k in range(steps):
         a_copy(1, k).start()
     late = [small(2, order_hbm, order_v), small(3, inv_hbm, inv_ref), small(4, order_hbm, order_s)]
-
-    barrier = pltpu.get_barrier_semaphore()
-
-    def greet(axis, me, n):
-        @pl.loop(1, n)
-        def _(d):
-            pl.semaphore_signal(barrier, inc=1, device_id={axis: lax.rem(me + d, n)}, device_id_type=MESH)
-
-    greet("gz", g, ng)
-    greet("row", r, nr)
-    greet("col", c, nc)
 
     def landed(ref, sem):
         pltpu.make_async_remote_copy(

time: 28 us -> 27.8 us (level)
  no operation moved by 1% of the time
where the time goes in v6:
time: 27.8 us; the launch traced here: 27.6 us
  Pallas kernels  27 us (97%)
  local copies, waits for them, and re-layouts  0.63 us (2%)
    pallas_call x1, Pallas kernels, on_device(): pl.pallas_call(functools.partial(kernel, ng, nr, nc, steps), out_shape=ja...  27 us
    unnamed x1, local copies, waits for them, and re-layouts  0.63 us

profile of v6, /device:TPU:68, one launch (start us, length us, event | category | flops | bytes accessed | tf_op | source)
XLA Modules:
  0.0 27.6 jit_solution(4253778634992009070)
XLA Ops:
  0.0 27.0 %shard_map.64 = f32[64,256]{1,0:T(8,128)S(1)} custom-call(bf16[1,512,8192]{2,1,0:T(8,128)(2,1)} %a_hbm.1, bf16[1,8192,256]{2,1,0:T(8,128)(2,1)} %b_hbm.1, s32[1,2,4]{2,1,0:T(2,128)} %bitcast.1, f32[64,256]{1,0:T(8,128)} %base_hbm.1, f32[2,256,256]{2,1,0:T(8,128)} %inv_hbm.1, s32[2,256]{1,0:T(2,128)} %order_hbm.1), custom_call_target="tpu_custom_call" | custom-call | tf_op jit(solution)/shard_map/pallas_call | solution.py:469
  27.0 0.6 %copy.8 = f32[64,256]{1,0:T(8,128)} copy(f32[64,256]{1,0:T(8,128)S(1)} %shard_map.64) | data formatting | bytes 131072

commit v7 on v6

--- a/solution.py
+++ b/solution.py
@@ -46,6 +46,7 @@
     mb = bs // mask_ref.shape[1]
     first = r == 0
     core = lax.rem(c, 2)
+    far_chips = sorted(range(2, nc), key=lambda d: -min(d // 2, (nc - d + 1) // 2))
     far_first = sorted(range(1, ng), key=lambda d: abs(2 * d - ng))
     others = jnp.logical_not(first)
     swap = jnp.where(first & (c == 0), 1, 0)
@@ -249,14 +250,13 @@
     def columns(m, only=None):
         @pl.when(c == 0 if m == 1 else others & (c == m // 2))
         def _():
-            @pl.loop(1 if m == 1 else 2, nc)
-            def _(d):
+            for d in ([1] if m == 1 else []) + far_chips:
                 if m == 1:
-                    pl.when(first | (d > 1))(lambda: column_copy(m, d).start())
+                    pl.when(first | (d > 1))(lambda d=d: column_copy(m, d).start())
                 elif only is None:
-                    column_copy(m, d, lax.rem(d, 2)).start()
-                else:
-                    pl.when(lax.rem(d, 2) == only)(lambda: column_copy(m, d, only).start())
+                    column_copy(m, d, d % 2).start()
+                elif d % 2 == only:
+                    column_copy(m, d, only).start()
 
     def columns_end(m):
         if m == 1:

time: 27.8 us -> 27.8 us (level)
  no operation moved by 1% of the time
where the time goes in v7:
time: 27.8 us; the launch traced here: 27.7 us
  Pallas kernels  27.1 us (97%)
  local copies, waits for them, and re-layouts  0.63 us (2%)
    pallas_call x1, Pallas kernels, on_device(): pl.pallas_call(functools.partial(kernel, ng, nr, nc, steps), out_shape=ja...  27.1 us
    unnamed x1, local copies, waits for them, and re-layouts  0.63 us

profile of v7, /device:TPU:68, one launch (start us, length us, event | category | flops | bytes accessed | tf_op | source)
XLA Modules:
  0.0 27.7 jit_solution(12461958012708324916)
XLA Ops:
  0.0 27.1 %shard_map.64 = f32[64,256]{1,0:T(8,128)S(1)} custom-call(bf16[1,512,8192]{2,1,0:T(8,128)(2,1)} %a_hbm.1, bf16[1,8192,256]{2,1,0:T(8,128)(2,1)} %b_hbm.1, s32[1,2,4]{2,1,0:T(2,128)} %bitcast.1, f32[64,256]{1,0:T(8,128)} %base_hbm.1, f32[2,256,256]{2,1,0:T(8,128)} %inv_hbm.1, s32[2,256]{1,0:T(2,128)} %order_hbm.1), custom_call_target="tpu_custom_call" | custom-call | tf_op jit(solution)/shard_map/pallas_call | solution.py:469
  27.1 0.6 %copy.8 = f32[64,256]{1,0:T(8,128)} copy(f32[64,256]{1,0:T(8,128)S(1)} %shard_map.64) | data formatting | bytes 131072
